TPU v7x, 512 devices: a whole 4x8x8 slice. The times are simulated.
512 devices in a mesh: lon: 64 (over y_hi, z, core), lat: 8 (over y_lo, x).
Axes of the slice: x: 4, y: 8 (y_hi: 4, y_lo: 2; y = y_hi * 2 + y_lo), z: 8, core: 2. Of those that a mesh axis runs over, the one named last changes fastest.
Arguments:
- state: bfloat16 [216, 8, 192, 1024], P(None, None, 'lon', 'lat'), may hold values from -6 to 6
- adjoint: bfloat16 [216, 8, 192, 1024], P(None, None, 'lon', 'lat'), may hold values from -6 to 6
- derivative: bfloat16 [3, 216, 216], replicated, may hold values from -0.25 to 0.25
- jac_tensor: bfloat16 [3, 8, 8, 8], replicated, may hold values from -2 to 2
- jac_offset: bfloat16 [3, 8, 8], replicated, may hold values from -2 to 2
- zonal_kernel: float32 [192], replicated, may hold values from -6 to 6
- face_numbers: int32 [192, 1024, 6], P('lon', 'lat'), may hold values from 0 to 5, each once within a row
- orientation: int32 [192, 1024, 6], P('lon', 'lat'), may hold values from 0 to 7
Outputs:
- gradient: bfloat16 [216, 8, 192, 1024], P(None, None, 'lon', 'lat')
Inputs may be any that keep to these rules, and one draw needn't show every extreme that they name: `face_numbers`: the six entries of each element are the local faces 0 to 5, each once.
All inputs are finite; a program needn't handle non-finite values.
Results may differ from a plain program's by a relative error of at most 0.0051.
Values may be sent and summed in bfloat16 or wider, within the bound.
A program may use at most 128 MiB of HBM per device.

v0:
```python
import functools

import jax
import jax.numpy as jnp
from jax import lax
from jax.experimental import pallas as pl
from jax.experimental.pallas import tpu as pltpu
from jax.sharding import PartitionSpec as P

MESH = pl.DeviceIdType.MESH
F32 = jnp.float32
BF16 = jnp.bfloat16
HIGH = lax.Precision.HIGHEST
STOPS = ((4, 0), (6, 1))
NETWORK = [(0, 5), (1, 3), (2, 4), (1, 2), (3, 4), (0, 3), (2, 5), (0, 1), (2, 3), (4, 5), (1, 2), (3, 4)]
VMEM_LIMIT = 56 * 1024 * 1024


def iota(shape, axis):
    return lax.broadcasted_iota(jnp.int32, shape, axis)


def onehot(condition):
    return condition.astype(F32).astype(BF16)


def fill_swaps(numbers_ref, swaps, wide):
    for t in range(3):
        keys = [jnp.broadcast_to(numbers_ref[t, g : g + 1, :], (8, 128)) for g in range(6)]
        for step, (i, j) in enumerate(NETWORK):
            swap = (keys[i] > keys[j]).astype(F32)
            swaps[t, step] = swap
            wide[t, step] = jnp.concatenate([swap, swap], axis=0).astype(BF16)
            keys[i], keys[j] = jnp.minimum(keys[i], keys[j]), jnp.maximum(keys[i], keys[j])


def face_node(face, u, v):
    if face < 2:
        return u * 36 + v * 6 + 5 * face
    if face < 4:
        return u * 36 + 30 * (face - 2) + v
    return 180 * (face - 4) + u * 6 + v


def select_own(s_ref, a_ref, wide, own):
    half = jnp.full((16, 128), 0.5, BF16)

    def step(index, carry):
        t = index // 6
        u = index % 6
        for v in range(6):
            parts = []
            for face in range(6):
                q = face_node(face, u, v)
                both = [s_ref[q, t].astype(F32), a_ref[q, t].astype(F32)]
                parts.append(jnp.concatenate(both, axis=0).astype(BF16))
            for s in range(len(NETWORK) - 1, -1, -1):
                i, j = NETWORK[s]
                swap = wide[t, s] > half
                parts[i], parts[j] = (
                    jnp.where(swap, parts[j], parts[i]),
                    jnp.where(swap, parts[i], parts[j]),
                )
            for g in range(6):
                own[g, t, u * 6 + v] = parts[g]
        return carry

    lax.fori_loop(0, 18, step, 0)


def weights(jac_ref, off_ref, wv, wf):
    x = jnp.dot(
        jac_ref[...], onehot((iota((8, 64), 1) & 7) == iota((8, 64), 0)), preferred_element_type=F32
    )
    row = iota((192, 64), 0)
    col = iota((192, 64), 1)
    x = jnp.where((col >> 3) == ((row >> 3) & 7), x, 0.0).astype(BF16)
    r = iota((24, 192), 0)
    k = iota((24, 192), 1)
    y = jnp.dot(
        onehot(((k >> 6) == (r >> 3)) & ((k & 7) == (r & 7))), x, preferred_element_type=F32
    )
    gb = onehot((iota((24, 8), 0) & 7) == iota((24, 8), 1))
    z = lax.dot_general(gb, off_ref[...], (((1,), (1,)), ((), ())), preferred_element_type=F32)
    z = jnp.where((iota((24, 24), 1) >> 3) == (iota((24, 24), 0) >> 3), z, 0.0).astype(BF16)
    fold = onehot((iota((24, 8), 0) & 7) == iota((24, 8), 1))
    lin = jnp.dot(z, fold, preferred_element_type=F32)
    sums = ((iota((32, 96), 1) - 64) >> 3 == iota((32, 96), 0) >> 3) & (iota((32, 96), 0) >= 8)
    for d in range(3):
        wf[d] = sums.astype(F32)
        wf[d, 0:8, 0:64] = y[d * 8 : d * 8 + 8]
        wf[d, 0:8, 64:72] = lin[d * 8 : d * 8 + 8]
    row = iota((64, 512), 0)
    col = iota((64, 512), 1)
    wide = jnp.dot(
        y.astype(BF16), onehot((row == (col & 63)) & (col < 448)), preferred_element_type=F32
    ) + jnp.dot(
        lin.astype(BF16),
        onehot((iota((8, 512), 0) == (iota((8, 512), 1) & 7)) & (iota((8, 512), 1) >= 448)),
        preferred_element_type=F32,
    )
    row = iota((8, 512), 0)
    col = iota((8, 512), 1)
    owner = jnp.where(col < 448, col >> 6, (col - 448) >> 3)
    keep = (owner == row) & (row < 7)
    for b in range(8):
        parts = [jnp.where(keep, wide[d * 8 + b : d * 8 + b + 1], 0.0) for d in range(3)]
        wv[b * 24 : b * 24 + 24, :] = jnp.concatenate(parts, axis=0)


def derivative_columns(d_ref, dperm):
    q = iota((216, 256), 0)
    col = iota((216, 256), 1)
    place = onehot((q == 7 * (col >> 3) + (col & 7)) & ((col & 7) < 7))
    for d in range(3):
        dperm[:, d * 256 : d * 256 + 256] = lax.dot_general(
            d_ref[d], place, (((0,), (0,)), ((), ())), preferred_element_type=F32
        ).astype(BF16)


def build_pairs(pair, s_ref, a_ref, prod):
    for half in range(2):
        for t in range(3):
            lanes = slice((half * 3 + t) * 128, (half * 3 + t) * 128 + 128)
            linear = []
            for q7 in range(7):
                q = jnp.minimum(pair * 14 + half * 7 + q7, 215)
                s = s_ref[q, t].astype(F32)
                a = a_ref[q, t].astype(F32)
                p = (a[:, None, :] * s[None, :, :]).reshape(64, 128)
                prod[q7 * 64 : q7 * 64 + 64, lanes] = p.astype(BF16)
                linear.append(a)
            prod[448:512, lanes] = jnp.concatenate(linear + linear[6:], axis=0).astype(BF16)


def contract_pairs(pair, wv, prod, trans):
    out = jnp.dot(wv[...].astype(BF16), prod[...], preferred_element_type=F32)
    for d in range(3):
        rows = pl.ds(pl.multiple_of(pair * 16 + d * 256, 16), 16)
        for b in range(8):
            part = out[b * 24 + d * 8 : b * 24 + d * 8 + 8]
            block = jnp.concatenate([part[:, 0:384], part[:, 384:768]], axis=0)
            trans[rows, b * 384 : b * 384 + 384] = block.astype(BF16)


def volume_steps(first, last, s_ref, a_ref, wv, prod_a, prod_b, trans):
    def step(index, carry):
        contract_pairs(2 * index, wv, prod_a, trans)
        build_pairs(2 * index + 1, s_ref, a_ref, prod_b)
        contract_pairs(2 * index + 1, wv, prod_b, trans)
        build_pairs(2 * index + 2, s_ref, a_ref, prod_a)
        return carry

    lax.fori_loop(first, last, step, 0)


def volume_product(dperm, trans, v_ref):
    for chunk in range(8):
        lanes = slice(chunk * 384, chunk * 384 + 384)
        out = jnp.dot(dperm[...], trans[:, lanes], preferred_element_type=F32)
        for t in range(3):
            v_ref[t, chunk * 216 : chunk * 216 + 216, :] = out[:, t * 128 : t * 128 + 128]


def zonal_matrix(kernel_ref, ring, y, z, c, chosen):
    ring[...] = jnp.zeros_like(ring)
    ring[:, 0:192] = jnp.broadcast_to(kernel_ref[...], (8, 192))
    twice = ring[...] + pltpu.roll(ring[...], 192, 1)
    full = jnp.broadcast_to(twice[0:1, :], (192, 384))
    circ = pltpu.roll(full, 0, 1, stride=1, stride_axis=0)[:, 0:192]
    row = iota((64, 192), 0)
    lon = iota((64, 192), 1)
    zr = (z + (row >> 3)) & 7
    ir = row & 7
    wanted = 48 * y + 6 * zr + 3 * c + ir
    pick = ((ir < 3) & (lon == wanted)).astype(F32)
    half = lax.dot_general(
        pick, circ, (((1,), (1,)), ((), ())), precision=HIGH, preferred_element_type=F32
    )
    eight = iota((8, 192), 1) >> 3
    ow = jnp.zeros_like(eight)
    for o in range(1, 8):
        ow = ow + (eight >= 3 * o).astype(jnp.int32)
    ic = eight - 3 * ow
    w = (2 * y + c - ow) & 7
    zc = (z - (iota((8, 192), 1) & 7)) & 7
    wanted = 48 * (w >> 1) + 6 * zc + 3 * (w & 1) + ic
    place = (iota((192, 192), 0) == wanted[0:1, :]).astype(F32)
    chosen[...] = jnp.dot(half, place, precision=HIGH, preferred_element_type=F32)


def flux(g, t, remote, own, turn_ref, wf, terms):
    code = jnp.broadcast_to(turn_ref[t, pl.ds(g, 1), :], (8, 128))
    half = jnp.full((16, 128), 0.5, BF16)
    bits = []
    for bit in (1, 2, 4):
        b = ((code & bit) != 0).astype(F32)
        bits.append(jnp.concatenate([b, b], axis=0).astype(BF16) > half)
    sigma = jnp.where(g % 2 == 0, -0.5, 0.5).astype(F32)
    matrix = wf[g // 2].astype(BF16)

    def swapped(tiles, mask, turn):
        return {n: jnp.where(mask, tiles[turn(n)], tiles[n]) for n in tiles}

    for orbits in (((0, 1),), ((0, 2),), ((1, 2),), ((0, 0), (1, 1), (2, 2))):
        inputs, jumps, lefts = [], [], []
        nodes = []
        for a, b in orbits:
            tiles = {}
            for u in (a, 5 - a):
                for v in (b, 5 - b):
                    tiles[u, v] = remote(t, u * 6 + v)
                    if (v, u) not in tiles:
                        tiles[v, u] = remote(t, v * 6 + u)
            tiles = swapped(tiles, bits[0], lambda n: (n[1], n[0]))
            tiles = swapped(tiles, bits[1], lambda n: (5 - n[0], n[1]))
            tiles = swapped(tiles, bits[2], lambda n: (n[0], 5 - n[1]))
            for n in tiles:
                m = n[0] * 6 + n[1]
                left = own[g, t, m].astype(F32)
                right = tiles[n].astype(F32)
                ul, wl, ur, wr = left[0:8], left[8:16], right[0:8], right[8:16]
                w = wl - wr
                prods = (w[:, None, :] * ul[None, :, :]).reshape(64, 128)
                rows = [prods, w, ul * ul, ur * ur, (ur - ul) * w]
                inputs.append(jnp.concatenate(rows, axis=0).astype(BF16))
                jumps.append(w)
                lefts.append(ul)
                nodes.append(m)
        summed = jnp.dot(matrix, jnp.concatenate(inputs, axis=1), preferred_element_type=F32)
        for k, m in enumerate(nodes):
            lanes = slice(k * 128, k * 128 + 128)
            sl = 1.0 + summed[8:16, lanes]
            sr = 1.0 + summed[16:24, lanes]
            inv = lax.rsqrt(sl)
            alpha = 0.25 * (sl * inv + jnp.sqrt(sr))
            terms[t, g, m] = (
                sigma * summed[0:8, lanes]
                + alpha * jumps[k]
                - (0.25 * summed[24:32, lanes] * inv) * lefts[k]
            )


def finish(swaps, terms, zon, v_ref, out_ref):
    def give_back(index, carry):
        t = index // 6
        u = index % 6
        for v in range(6):
            m = u * 6 + v
            parts = [terms[t, g, m] for g in range(6)]
            for s, (i, j) in enumerate(NETWORK):
                swap = swaps[t, s] > 0.5
                parts[i], parts[j] = (
                    jnp.where(swap, parts[j], parts[i]),
                    jnp.where(swap, parts[i], parts[j]),
                )
            for face in range(6):
                terms[t, face, m] = parts[face]
        return carry

    lax.fori_loop(0, 18, give_back, 0)

    def total(t, carry):
        zon_t = zon[pl.ds(t, 8, stride=8), :]
        for k in range(6):
            for j in range(6):
                for i in range(6):
                    p = k * 36 + j * 6 + i
                    acc = v_ref[t, pl.ds(p, 8, stride=216), :] + zon_t
                    if i in (0, 5):
                        acc = acc + terms[t, i // 5, k * 6 + j]
                    if j in (0, 5):
                        acc = acc + terms[t, 2 + j // 5, k * 6 + i]
                    if k in (0, 5):
                        acc = acc + terms[t, 4 + k // 5, j * 6 + i]
                    out_ref[p, t] = acc.astype(BF16)
        return carry

    lax.fori_loop(0, 3, total, 0)


def kernel(
    s_ref, a_ref, d_ref, jac_ref, off_ref, kernel_ref, numbers_ref, turn_ref, out_ref,
    own, v_ref, rlon, rs, rn, swaps, wide, wv, wf, dperm, prod_a, prod_b, trans,
    ring, chosen, msend, mgot, gath, zout, zrecv, terms,
    send_h, recv_h, send_1, recv_1, send_2, recv_2, send_3, recv_3,
):
    lon = lax.axis_index("lon")
    lat = lax.axis_index("lat")
    y = lon // 16
    z = (lon // 2) % 8
    c = lon % 2
    w = 2 * y + c

    def lon_of(y, z, c):
        return (y * 8 + z) * 2 + c

    along_z = [lon_of(y, (z + o) % 8, c) for o in range(1, 8)]
    around = []
    for o in range(1, 8):
        other = (w + o) % 8
        around.append(lon_of(other // 2, z, other % 2))
    west, east = (lon + 63) % 64, (lon + 1) % 64
    south, north = (lat + 7) % 8, (lat + 1) % 8

    barrier = pltpu.get_barrier_semaphore()
    for target in along_z + around + [west, east]:
        pl.semaphore_signal(barrier, inc=1, device_id={"lon": target}, device_id_type=MESH)
    for target in (south, north):
        pl.semaphore_signal(barrier, inc=1, device_id={"lat": target}, device_id_type=MESH)

    def copy(src, dst, send, recv, where):
        return pltpu.make_async_remote_copy(
            src_ref=src, dst_ref=dst, send_sem=send, recv_sem=recv, device_id=where, device_id_type=MESH
        )

    def volume(first, last):
        volume_steps(first, last, s_ref, a_ref, wv, prod_a, prod_b, trans)

    msend[...] = jnp.zeros_like(msend)

    def add(q, totals):
        totals = list(totals)
        for r in range(8):
            for t in range(3):
                totals[t] = totals[t] + a_ref[q * 8 + r, t].astype(F32)
        return tuple(totals)

    totals = lax.fori_loop(0, 27, add, (jnp.zeros((8, 128), F32),) * 3)
    for t in range(3):
        msend[pl.ds(t, 8, stride=8), :] = totals[t] / 216.0
    fill_swaps(numbers_ref, swaps, wide)
    select_own(s_ref, a_ref, wide, own)
    weights(jac_ref, off_ref, wv, wf)
    zonal_matrix(kernel_ref, ring, y, z, c, chosen)
    derivative_columns(d_ref, dperm)
    build_pairs(0, s_ref, a_ref, prod_a)
    early = z == 0
    stops = [jnp.where(early, e, n) for e, n in STOPS]
    volume(0, stops[0])
    pl.semaphore_wait(barrier, 18)

    hops = []
    for o in range(1, 8):
        start = pl.multiple_of(((z + o) % 8) * 8, 8)
        hops.append(
            copy(
                msend.at[pl.ds(start, 8)], mgot.at[o * 8 : o * 8 + 8], send_1.at[o], recv_1.at[o],
                {"lon": along_z[o - 1]},
            )
        )
    for hop in hops:
        hop.start()
    halos = [
        copy(own.at[1, 2], rlon.at[0], send_h.at[0], recv_h.at[0], {"lon": east}),
        copy(own.at[0, 0], rlon.at[1], send_h.at[1], recv_h.at[1], {"lon": west}),
        copy(own.at[3], rs, send_h.at[2], recv_h.at[2], {"lat": north}),
        copy(own.at[2], rn, send_h.at[3], recv_h.at[3], {"lat": south}),
    ]
    for halo in halos:
        halo.start()
    mgot[0:8] = msend[pl.ds(pl.multiple_of(z * 8, 8), 8), :]
    volume(stops[0], stops[1])
    for hop in hops:
        hop.wait_recv()
    for i in range(3):
        gath[0, i * 8 : i * 8 + 8] = mgot[pl.ds(i, 8, stride=8), :]
    spread = [
        copy(gath.at[0], gath.at[o], send_2.at[o], recv_2.at[o], {"lon": around[o - 1]})
        for o in range(1, 8)
    ]
    for hop in spread:
        hop.start()
    volume(stops[1], 8)
    volume_product(dperm, trans, v_ref)
    for hop in spread:
        hop.wait_recv()
    zout[...] = jnp.dot(
        chosen[...], gath[...].reshape(192, 128), precision=HIGH, preferred_element_type=F32
    )
    place = pl.ds(pl.multiple_of(z * 8, 8), 8)
    back = [
        copy(
            zout.at[o * 8 : o * 8 + 8], zrecv.at[place], send_3.at[o], recv_3.at[o],
            {"lon": along_z[o - 1]},
        )
        for o in range(1, 8)
    ]
    for hop in back:
        hop.start()
    zrecv[place, :] = zout[0:8, :]

    lane = iota((16, 128), 1)
    zero = jnp.zeros((16, 128), BF16)
    inner = (lane & 63).astype(F32).astype(BF16)
    below_first = inner < jnp.full((16, 128), 0.5, BF16)
    above_last = inner > jnp.full((16, 128), 62.5, BF16)
    upper = lane.astype(F32).astype(BF16) > jnp.full((16, 128), 63.5, BF16)

    def faces(g, t, remote):
        flux(g, t, remote, own, turn_ref, wf, terms)

    def from_below(t, m):
        return jnp.where(below_first, zero, pltpu.roll(own[5, t, m], 1, 1))

    def from_above(t, m):
        return jnp.where(above_last, zero, pltpu.roll(own[4, t, m], 127, 1))

    def radial(t, carry):
        faces(4, t, from_below)
        faces(5, t, from_above)
        return carry

    lax.fori_loop(0, 3, radial, 0)

    def inner_lon(index, carry):
        g = index // 2
        faces(g, index % 2 + 1 - g, lambda t, m: own[1 - g, t - 1 + 2 * g, m])
        return carry

    lax.fori_loop(0, 4, inner_lon, 0)
    halos[0].wait_recv()
    halos[1].wait_recv()

    def outer_lon(g, carry):
        faces(g, 2 * g, lambda t, m: rlon[g, m])
        return carry

    lax.fori_loop(0, 2, outer_lon, 0)
    halos[2].wait_recv()
    halos[3].wait_recv()
    has_south = jnp.broadcast_to(jnp.where(lat > 0, 1.0, 0.0).astype(F32), (16, 128)).astype(BF16)
    has_north = jnp.broadcast_to(jnp.where(lat < 7, 1.0, 0.0).astype(F32), (16, 128)).astype(BF16)

    def from_south(t, m):
        return pltpu.roll(jnp.where(upper, rs[t, m] * has_south, own[3, t, m]), 64, 1)

    def from_north(t, m):
        return pltpu.roll(jnp.where(upper, own[2, t, m], rn[t, m] * has_north), 64, 1)

    def lats(t, carry):
        faces(2, t, from_south)
        faces(3, t, from_north)
        return carry

    lax.fori_loop(0, 3, lats, 0)
    for hop in back:
        hop.wait_recv()
    finish(swaps, terms, zrecv, v_ref, out_ref)
    for sent in hops + halos + spread + back:
        sent.wait_send()


def whole(*operands):
    vmem = pl.BlockSpec(memory_space=pltpu.VMEM)
    dma = pltpu.SemaphoreType.DMA
    return pl.pallas_call(
        kernel,
        out_shape=jax.ShapeDtypeStruct((216, 3, 8, 128), BF16),
        in_specs=[vmem] * 8,
        out_specs=vmem,
        scratch_shapes=[
            pltpu.VMEM((6, 3, 36, 16, 128), BF16),
            pltpu.VMEM((3, 1728, 128), F32),
            pltpu.VMEM((2, 36, 16, 128), BF16),
            pltpu.VMEM((3, 36, 16, 128), BF16),
            pltpu.VMEM((3, 36, 16, 128), BF16),
            pltpu.VMEM((3, 12, 8, 128), F32),
            pltpu.VMEM((3, 12, 16, 128), BF16),
            pltpu.VMEM((192, 512), F32),
            pltpu.VMEM((3, 32, 96), F32),
            pltpu.VMEM((216, 768), BF16),
            pltpu.VMEM((512, 768), BF16),
            pltpu.VMEM((512, 768), BF16),
            pltpu.VMEM((768, 3072), BF16),
            pltpu.VMEM((8, 384), F32),
            pltpu.VMEM((64, 192), F32),
            pltpu.VMEM((64, 128), F32),
            pltpu.VMEM((64, 128), F32),
            pltpu.VMEM((8, 24, 128), F32),
            pltpu.VMEM((64, 128), F32),
            pltpu.VMEM((64, 128), F32),
            pltpu.VMEM((3, 6, 36, 8, 128), F32),
            dma((4,)), dma((4,)), dma((8,)), dma((8,)), dma((8,)), dma((8,)), dma((8,)), dma((8,)),
        ],
        compiler_params=pltpu.CompilerParams(
            collective_id=0, has_side_effects=True, vmem_limit_bytes=VMEM_LIMIT
        ),
    )(*operands)


def body(state, adjoint, derivative, jac_tensor, jac_offset, zonal_kernel, face_numbers, orientation):
    s = jnp.transpose(state, (0, 2, 1, 3))
    a = jnp.transpose(adjoint, (0, 2, 1, 3))
    jac = jac_tensor.reshape(192, 8)
    off = jac_offset.reshape(24, 8)
    ring = zonal_kernel.reshape(1, 192)
    numbers = jnp.transpose(face_numbers, (0, 2, 1))
    turnings = jnp.transpose(orientation, (0, 2, 1))
    out = whole(s, a, derivative, jac, off, ring, numbers, turnings)
    return jnp.transpose(out, (0, 2, 1, 3))


def solution(mesh):
    in_specs = (
        P(None, None, "lon", "lat"),
        P(None, None, "lon", "lat"),
        P(),
        P(),
        P(),
        P(),
        P("lon", "lat", None),
        P("lon", "lat", None),
    )
    out_specs = P(None, None, "lon", "lat")
    return jax.shard_map(body, mesh=mesh, in_specs=in_specs, out_specs=out_specs, check_vma=False)
```

profile of v0, /device:TPU:15, one launch (start us, length us, event | category | flops | bytes accessed | tf_op | source)
XLA Modules:
  0.0 45.6 jit_solution(556905712784024256)
XLA Ops:
  0.0 43.0 %shard_map.82 = bf16[216,3,8,128]{3,2,1,0:T(8,128)(2,1)} custom-call(bf16[216,3,8,128]{3,2,1,0:T(8,128)(2,1)} %bitcast.9, bf16[216,3,8,128]{3,2,1,0:T(8,128)(2,1)} %bitcast.10, bf16[3,216,216]{2,1,0:T(8,128)(2,1)} %d_ref.1, bf16[192,8]{1,0:T(8,128)(2,1)} %bitcast.11, bf16[24,8]{1,0:T(8,128)(2,1)} %bitcast.14, f32[1,192]{1,0:T(1,128)} %bitcast.15, ...), custom_call_target="tpu_custom_call" | custom-call | tf_op jit(solution)/shard_map/pallas_call | solution.py:457
  43.0 2.6 %copy.10 = bf16[216,8,3,128]{3,1,2,0:T(8,128)(2,1)} copy(bf16[216,8,3,128]{3,1,2,0:T(8,128)(2,1)} %bitcast.8) | data formatting | bytes 2654208
where the time goes:
time: 45.8 us; the launch traced here: 45.6 us
  Pallas kernels  43 us (94%)
  local copies, waits for them, and re-layouts  2.61 us (6%)
    pallas_call x1, Pallas kernels, whole(): pl.pallas_call(kernel, out_shape=jax.ShapeDtypeStruct((216, 3, 8, 128), B...  43 us
    unnamed x1, local copies, waits for them, and re-layouts  2.61 us

commit v1 on v0

--- a/solution.py
+++ b/solution.py
@@ -11,7 +11,7 @@
 F32 = jnp.float32
 BF16 = jnp.bfloat16
 HIGH = lax.Precision.HIGHEST
-STOPS = ((4, 0), (6, 1))
+STOPS = ((1, 0), (6, 1), (8, 5))
 NETWORK = [(0, 5), (1, 3), (2, 4), (1, 2), (3, 4), (0, 3), (2, 5), (0, 1), (2, 3), (4, 5), (1, 2), (3, 4)]
 VMEM_LIMIT = 56 * 1024 * 1024
 
@@ -281,7 +281,7 @@
 
 def kernel(
     s_ref, a_ref, d_ref, jac_ref, off_ref, kernel_ref, numbers_ref, turn_ref, out_ref,
-    own, v_ref, rlon, rs, rn, swaps, wide, wv, wf, dperm, prod_a, prod_b, trans,
+    own, v_ref, rlon, to_north, to_south, rs, rn, swaps, wide, wv, wf, dperm, prod_a, prod_b, trans,
     ring, chosen, msend, mgot, gath, zout, zrecv, terms,
     send_h, recv_h, send_1, recv_1, send_2, recv_2, send_3, recv_3,
 ):
@@ -329,15 +329,58 @@
     totals = lax.fori_loop(0, 27, add, (jnp.zeros((8, 128), F32),) * 3)
     for t in range(3):
         msend[pl.ds(t, 8, stride=8), :] = totals[t] / 216.0
+    lane = iota((16, 128), 1)
+    zero = jnp.zeros((16, 128), BF16)
+    inner = (lane & 63).astype(F32).astype(BF16)
+    below_first = inner < jnp.full((16, 128), 0.5, BF16)
+    above_last = inner > jnp.full((16, 128), 62.5, BF16)
+    upper = lane.astype(F32).astype(BF16) > jnp.full((16, 128), 63.5, BF16)
+
     fill_swaps(numbers_ref, swaps, wide)
     select_own(s_ref, a_ref, wide, own)
-    weights(jac_ref, off_ref, wv, wf)
-    zonal_matrix(kernel_ref, ring, y, z, c, chosen)
-    derivative_columns(d_ref, dperm)
-    build_pairs(0, s_ref, a_ref, prod_a)
+
+    def pack(index, carry):
+        t = index // 3
+        for v in range(6):
+            m = (index % 3) * 6 + v
+            to_north[t, m] = jnp.where(upper, own[3, t, m], pltpu.roll(own[3, t, m + 18], 64, 1))
+            to_south[t, m] = jnp.where(upper, pltpu.roll(own[2, t, m + 18], 64, 1), own[2, t, m])
+        return carry
+
+    lax.fori_loop(0, 9, pack, 0)
+    has_north = lat < 7
+    has_south = lat > 0
+
+    def blank(ref):
+        def step(m, carry):
+            for t in range(3):
+                ref[t, m] = zero
+            return carry
+
+        lax.fori_loop(0, 18, step, 0)
+
+    @pl.when(lat == 7)
+    def _():
+        blank(rn)
+
+    @pl.when(lat == 0)
+    def _():
+        blank(rs)
+
+    def prepare():
+        weights(jac_ref, off_ref, wv, wf)
+        zonal_matrix(kernel_ref, ring, y, z, c, chosen)
+        derivative_columns(d_ref, dperm)
+        build_pairs(0, s_ref, a_ref, prod_a)
+
     early = z == 0
     stops = [jnp.where(early, e, n) for e, n in STOPS]
-    volume(0, stops[0])
+
+    @pl.when(early)
+    def _():
+        prepare()
+        volume(0, STOPS[0][0])
+
     pl.semaphore_wait(barrier, 18)
 
     hops = []
@@ -354,12 +397,26 @@
     halos = [
         copy(own.at[1, 2], rlon.at[0], send_h.at[0], recv_h.at[0], {"lon": east}),
         copy(own.at[0, 0], rlon.at[1], send_h.at[1], recv_h.at[1], {"lon": west}),
-        copy(own.at[3], rs, send_h.at[2], recv_h.at[2], {"lat": north}),
-        copy(own.at[2], rn, send_h.at[3], recv_h.at[3], {"lat": south}),
     ]
+    northward = copy(to_north, rs, send_h.at[2], recv_h.at[2], {"lat": north})
+    southward = copy(to_south, rn, send_h.at[3], recv_h.at[3], {"lat": south})
     for halo in halos:
         halo.start()
+
+    @pl.when(has_north)
+    def _():
+        northward.start()
+
+    @pl.when(has_south)
+    def _():
+        southward.start()
+
     mgot[0:8] = msend[pl.ds(pl.multiple_of(z * 8, 8), 8), :]
+
+    @pl.when(jnp.logical_not(early))
+    def _():
+        prepare()
+
     volume(stops[0], stops[1])
     for hop in hops:
         hop.wait_recv()
@@ -371,8 +428,7 @@
     ]
     for hop in spread:
         hop.start()
-    volume(stops[1], 8)
-    volume_product(dperm, trans, v_ref)
+    volume(stops[1], stops[2])
     for hop in spread:
         hop.wait_recv()
     zout[...] = jnp.dot(
@@ -389,13 +445,8 @@
     for hop in back:
         hop.start()
     zrecv[place, :] = zout[0:8, :]
-
-    lane = iota((16, 128), 1)
-    zero = jnp.zeros((16, 128), BF16)
-    inner = (lane & 63).astype(F32).astype(BF16)
-    below_first = inner < jnp.full((16, 128), 0.5, BF16)
-    above_last = inner > jnp.full((16, 128), 62.5, BF16)
-    upper = lane.astype(F32).astype(BF16) > jnp.full((16, 128), 63.5, BF16)
+    volume(stops[2], 8)
+    volume_product(dperm, trans, v_ref)
 
     def faces(g, t, remote):
         flux(g, t, remote, own, turn_ref, wf, terms)
@@ -427,16 +478,24 @@
         return carry
 
     lax.fori_loop(0, 2, outer_lon, 0)
-    halos[2].wait_recv()
-    halos[3].wait_recv()
-    has_south = jnp.broadcast_to(jnp.where(lat > 0, 1.0, 0.0).astype(F32), (16, 128)).astype(BF16)
-    has_north = jnp.broadcast_to(jnp.where(lat < 7, 1.0, 0.0).astype(F32), (16, 128)).astype(BF16)
+
+    @pl.when(has_south)
+    def _():
+        northward.wait_recv()
+
+    @pl.when(has_north)
+    def _():
+        southward.wait_recv()
 
     def from_south(t, m):
-        return pltpu.roll(jnp.where(upper, rs[t, m] * has_south, own[3, t, m]), 64, 1)
+        if m < 18:
+            return pltpu.roll(jnp.where(upper, rs[t, m], own[3, t, m]), 64, 1)
+        return jnp.where(upper, pltpu.roll(own[3, t, m], 64, 1), rs[t, m - 18])
 
     def from_north(t, m):
-        return pltpu.roll(jnp.where(upper, own[2, t, m], rn[t, m] * has_north), 64, 1)
+        if m < 18:
+            return pltpu.roll(jnp.where(upper, own[2, t, m], rn[t, m]), 64, 1)
+        return jnp.where(upper, rn[t, m - 18], pltpu.roll(own[2, t, m], 64, 1))
 
     def lats(t, carry):
         faces(2, t, from_south)
@@ -449,6 +508,14 @@
     finish(swaps, terms, zrecv, v_ref, out_ref)
     for sent in hops + halos + spread + back:
         sent.wait_send()
+
+    @pl.when(has_north)
+    def _():
+        northward.wait_send()
+
+    @pl.when(has_south)
+    def _():
+        southward.wait_send()
 
 
 def whole(*operands):
@@ -463,8 +530,10 @@
             pltpu.VMEM((6, 3, 36, 16, 128), BF16),
             pltpu.VMEM((3, 1728, 128), F32),
             pltpu.VMEM((2, 36, 16, 128), BF16),
-            pltpu.VMEM((3, 36, 16, 128), BF16),
-            pltpu.VMEM((3, 36, 16, 128), BF16),
+            pltpu.VMEM((3, 18, 16, 128), BF16),
+            pltpu.VMEM((3, 18, 16, 128), BF16),
+            pltpu.VMEM((3, 18, 16, 128), BF16),
+            pltpu.VMEM((3, 18, 16, 128), BF16),
             pltpu.VMEM((3, 12, 8, 128), F32),
             pltpu.VMEM((3, 12, 16, 128), BF16),
             pltpu.VMEM((192, 512), F32),

time: 45.8 us -> 42.8 us (0.934)
  the two profiles are of different devices: /device:TPU:15 before, /device:TPU:9 now
where the time goes in v1:
time: 42.8 us; the launch traced here: 42.7 us
  Pallas kernels  40 us (93%)
  local copies, waits for them, and re-layouts  2.61 us (6%)
    pallas_call x1, Pallas kernels, whole(): pl.pallas_call(kernel, out_shape=jax.ShapeDtypeStruct((216, 3, 8, 128), B...  40 us
    unnamed x1, local copies, waits for them, and re-layouts  2.61 us

profile of v1, /device:TPU:9, one launch (start us, length us, event | category | flops | bytes accessed | tf_op | source)
XLA Modules:
  0.0 42.7 jit_solution(11729610576142420409)
XLA Ops:
  0.0 40.0 %shard_map.82 = bf16[216,3,8,128]{3,2,1,0:T(8,128)(2,1)} custom-call(bf16[216,3,8,128]{3,2,1,0:T(8,128)(2,1)} %bitcast.9, bf16[216,3,8,128]{3,2,1,0:T(8,128)(2,1)} %bitcast.10, bf16[3,216,216]{2,1,0:T(8,128)(2,1)} %d_ref.1, bf16[192,8]{1,0:T(8,128)(2,1)} %bitcast.11, bf16[24,8]{1,0:T(8,128)(2,1)} %bitcast.14, f32[1,192]{1,0:T(1,128)} %bitcast.15, ...), custom_call_target="tpu_custom_call" | custom-call | tf_op jit(solution)/shard_map/pallas_call | solution.py:524
  40.0 2.6 %copy.10 = bf16[216,8,3,128]{3,1,2,0:T(8,128)(2,1)} copy(bf16[216,8,3,128]{3,1,2,0:T(8,128)(2,1)} %bitcast.8) | data formatting | bytes 2654208

commit v2 on v1

--- a/solution.py
+++ b/solution.py
@@ -11,9 +11,9 @@
 F32 = jnp.float32
 BF16 = jnp.bfloat16
 HIGH = lax.Precision.HIGHEST
-STOPS = ((1, 0), (6, 1), (8, 5))
 NETWORK = [(0, 5), (1, 3), (2, 4), (1, 2), (3, 4), (0, 3), (2, 5), (0, 1), (2, 3), (4, 5), (1, 2), (3, 4)]
-VMEM_LIMIT = 56 * 1024 * 1024
+VMEM_LIMIT = 30 * 1024 * 1024
+FINISH_LIMIT = 20 * 1024 * 1024
 
 
 def iota(shape, axis):
@@ -241,13 +241,13 @@
             )
 
 
-def finish(swaps, terms, zon, v_ref, out_ref):
+def finish(swaps, given, terms, zon, v_ref, out_ref):
     def give_back(index, carry):
         t = index // 6
         u = index % 6
         for v in range(6):
             m = u * 6 + v
-            parts = [terms[t, g, m] for g in range(6)]
+            parts = [given[t, g, m] for g in range(6)]
             for s, (i, j) in enumerate(NETWORK):
                 swap = swaps[t, s] > 0.5
                 parts[i], parts[j] = (
@@ -280,10 +280,11 @@
 
 
 def kernel(
-    s_ref, a_ref, d_ref, jac_ref, off_ref, kernel_ref, numbers_ref, turn_ref, out_ref,
-    own, v_ref, rlon, to_north, to_south, rs, rn, swaps, wide, wv, wf, dperm, prod_a, prod_b, trans,
-    ring, chosen, msend, mgot, gath, zout, zrecv, terms,
-    send_h, recv_h, send_1, recv_1, send_2, recv_2, send_3, recv_3,
+    s_hbm, a_hbm, d_ref, jac_ref, off_ref, kernel_ref, numbers_ref, turn_ref,
+    terms, v_ref, zon_ref, swaps,
+    s_ref, a_ref, own, rlon, to_north, to_south, rs, rn, wide, wv, wf, dperm, prod_a, prod_b, trans,
+    ring, chosen, msend, mgot, gath, zout, zrecv,
+    load, send_h, recv_h, send_1, recv_1, send_2, recv_2, send_3, recv_3,
 ):
     lon = lax.axis_index("lon")
     lat = lax.axis_index("lat")
@@ -316,6 +317,17 @@
 
     def volume(first, last):
         volume_steps(first, last, s_ref, a_ref, wv, prod_a, prod_b, trans)
+
+    loads = [
+        pltpu.make_async_copy(a_hbm, a_ref, load.at[0]),
+        pltpu.make_async_copy(s_hbm, s_ref, load.at[1]),
+    ]
+    for each in loads:
+        each.start()
+    zonal_matrix(kernel_ref, ring, y, z, c, chosen)
+    derivative_columns(d_ref, dperm)
+    fill_swaps(numbers_ref, swaps, wide)
+    loads[0].wait()
 
     msend[...] = jnp.zeros_like(msend)
 
@@ -336,7 +348,7 @@
     above_last = inner > jnp.full((16, 128), 62.5, BF16)
     upper = lane.astype(F32).astype(BF16) > jnp.full((16, 128), 63.5, BF16)
 
-    fill_swaps(numbers_ref, swaps, wide)
+    loads[1].wait()
     select_own(s_ref, a_ref, wide, own)
 
     def pack(index, carry):
@@ -369,17 +381,19 @@
 
     def prepare():
         weights(jac_ref, off_ref, wv, wf)
-        zonal_matrix(kernel_ref, ring, y, z, c, chosen)
-        derivative_columns(d_ref, dperm)
         build_pairs(0, s_ref, a_ref, prod_a)
 
-    early = z == 0
-    stops = [jnp.where(early, e, n) for e, n in STOPS]
+    early = z < 4
+    stops = [
+        jnp.where(early, jnp.where(z == 3, 1, 5 - z), 0),
+        jnp.where(early, jnp.where(z < 2, 8, 6), 2),
+        jnp.where(early, 8, 6),
+    ]
 
     @pl.when(early)
     def _():
         prepare()
-        volume(0, STOPS[0][0])
+        volume(0, stops[0])
 
     pl.semaphore_wait(barrier, 18)
 
@@ -429,6 +443,11 @@
     for hop in spread:
         hop.start()
     volume(stops[1], stops[2])
+
+    @pl.when(early)
+    def _():
+        volume_product(dperm, trans, v_ref)
+
     for hop in spread:
         hop.wait_recv()
     zout[...] = jnp.dot(
@@ -445,8 +464,10 @@
     for hop in back:
         hop.start()
     zrecv[place, :] = zout[0:8, :]
-    volume(stops[2], 8)
-    volume_product(dperm, trans, v_ref)
+    @pl.when(jnp.logical_not(early))
+    def _():
+        volume(stops[2], 8)
+        volume_product(dperm, trans, v_ref)
 
     def faces(g, t, remote):
         flux(g, t, remote, own, turn_ref, wf, terms)
@@ -505,7 +526,7 @@
     lax.fori_loop(0, 3, lats, 0)
     for hop in back:
         hop.wait_recv()
-    finish(swaps, terms, zrecv, v_ref, out_ref)
+    zon_ref[...] = zrecv[...]
     for sent in hops + halos + spread + back:
         sent.wait_send()
 
@@ -518,23 +539,28 @@
         southward.wait_send()
 
 
-def whole(*operands):
+def exchange(*operands):
     vmem = pl.BlockSpec(memory_space=pltpu.VMEM)
     dma = pltpu.SemaphoreType.DMA
     return pl.pallas_call(
         kernel,
-        out_shape=jax.ShapeDtypeStruct((216, 3, 8, 128), BF16),
-        in_specs=[vmem] * 8,
-        out_specs=vmem,
+        out_shape=[
+            jax.ShapeDtypeStruct((3, 6, 36, 8, 128), F32),
+            jax.ShapeDtypeStruct((3, 1728, 128), F32),
+            jax.ShapeDtypeStruct((64, 128), F32),
+            jax.ShapeDtypeStruct((3, 12, 8, 128), F32),
+        ],
+        in_specs=[pl.BlockSpec(memory_space=pltpu.HBM)] * 2 + [vmem] * 6,
+        out_specs=[vmem] * 4,
         scratch_shapes=[
+            pltpu.VMEM((216, 3, 8, 128), BF16),
+            pltpu.VMEM((216, 3, 8, 128), BF16),
             pltpu.VMEM((6, 3, 36, 16, 128), BF16),
-            pltpu.VMEM((3, 1728, 128), F32),
             pltpu.VMEM((2, 36, 16, 128), BF16),
             pltpu.VMEM((3, 18, 16, 128), BF16),
             pltpu.VMEM((3, 18, 16, 128), BF16),
             pltpu.VMEM((3, 18, 16, 128), BF16),
             pltpu.VMEM((3, 18, 16, 128), BF16),
-            pltpu.VMEM((3, 12, 8, 128), F32),
             pltpu.VMEM((3, 12, 16, 128), BF16),
             pltpu.VMEM((192, 512), F32),
             pltpu.VMEM((3, 32, 96), F32),
@@ -549,12 +575,27 @@
             pltpu.VMEM((8, 24, 128), F32),
             pltpu.VMEM((64, 128), F32),
             pltpu.VMEM((64, 128), F32),
-            pltpu.VMEM((3, 6, 36, 8, 128), F32),
-            dma((4,)), dma((4,)), dma((8,)), dma((8,)), dma((8,)), dma((8,)), dma((8,)), dma((8,)),
+            dma((2,)), dma((4,)), dma((4,)), dma((8,)), dma((8,)), dma((8,)), dma((8,)), dma((8,)), dma((8,)),
         ],
         compiler_params=pltpu.CompilerParams(
             collective_id=0, has_side_effects=True, vmem_limit_bytes=VMEM_LIMIT
         ),
+    )(*operands)
+
+
+def finish_kernel(terms_in, v_ref, zon_ref, swaps, out_ref, terms):
+    finish(swaps, terms_in, terms, zon_ref, v_ref, out_ref)
+
+
+def finished(*operands):
+    vmem = pl.BlockSpec(memory_space=pltpu.VMEM)
+    return pl.pallas_call(
+        finish_kernel,
+        out_shape=jax.ShapeDtypeStruct((216, 3, 8, 128), BF16),
+        in_specs=[vmem] * 4,
+        out_specs=vmem,
+        scratch_shapes=[pltpu.VMEM((3, 6, 36, 8, 128), F32)],
+        compiler_params=pltpu.CompilerParams(vmem_limit_bytes=FINISH_LIMIT),
     )(*operands)
 
 
@@ -566,7 +607,12 @@
     ring = zonal_kernel.reshape(1, 192)
     numbers = jnp.transpose(face_numbers, (0, 2, 1))
     turnings = jnp.transpose(orientation, (0, 2, 1))
-    out = whole(s, a, derivative, jac, off, ring, numbers, turnings)
+    s, a, derivative, jac, off, ring, numbers, turnings = [
+        pltpu.with_memory_space_constraint(x, pltpu.HBM)
+        for x in (s, a, derivative, jac, off, ring, numbers, turnings)
+    ]
+    parts = exchange(s, a, derivative, jac, off, ring, numbers, turnings)
+    out = finished(*parts)
     return jnp.transpose(out, (0, 2, 1, 3))
 
 

time: 42.8 us -> 38.1 us (0.89)
  the two profiles are of different devices: /device:TPU:9 before, /device:TPU:1 now
where the time goes in v2:
time: 38.1 us; the launch traced here: 37.9 us
  Pallas kernels  37.9 us (99%)
    pallas_call x1, Pallas kernels, exchange(): pl.pallas_call(kernel, out_shape=[jax.ShapeDtypeStruct((3, 6, 36, 8, 128)...  35.6 us
    pallas_call x1, Pallas kernels, finished(): pl.pallas_call(finish_kernel, out_shape=jax.ShapeDtypeStruct((216, 3, 8,...  2.33 us

profile of v2, /device:TPU:1, one launch (start us, length us, event | category | flops | bytes accessed | tf_op | source)
XLA Modules:
  0.0 37.9 jit_solution(18415270888696283470)
XLA Ops:
  0.0 35.6 %shard_map.82 = (f32[3,6,36,8,128]{4,3,2,1,0:T(8,128)S(1)}, f32[3,1728,128]{2,1,0:T(8,128)S(1)}, f32[64,128]{1,0:T(8,128)S(1)}, f32[3,12,8,128]{3,2,1,0:T(8,128)S(1)}) custom-call(bf16[216,3,8,128]{3,2,1,0:T(8,128)(2,1)} %bitcast.8, bf16[216,3,8,128]{3,2,1,0:T(8,128)(2,1)} %bitcast.9, bf16[3,216,216]{2,1,0:T(8,128)(2,1)} %d_ref.1, bf16[192,8]{1,0:T(8,128)(2,1)} %bitcast.10, ...), custom_call_target="tpu_custom_call" | custom-call | tf_op jit(solution)/shard_map/pallas_call | solution.py:545
  35.6 2.3 %shard_map.83 = bf16[216,3,8,128]{3,2,1,0:T(8,128)(2,1)} custom-call(f32[3,6,36,8,128]{4,3,2,1,0:T(8,128)S(1)} %get-tuple-element.9.terms_in, f32[3,1728,128]{2,1,0:T(8,128)S(1)} %get-tuple-element.10.v_ref, f32[64,128]{1,0:T(8,128)S(1)} %get-tuple-element.11.zon_ref, f32[3,12,8,128]{3,2,1,0:T(8,128)S(1)} %get-tuple-element.12.swaps), custom_call_target="tpu_custom_call" | custom-call | tf_op jit(solution)/shard_map/pallas_call | solution.py:592

commit v3 on v2

--- a/solution.py
+++ b/solution.py
@@ -127,8 +127,11 @@
                 q = jnp.minimum(pair * 14 + half * 7 + q7, 215)
                 s = s_ref[q, t].astype(F32)
                 a = a_ref[q, t].astype(F32)
-                p = (a[:, None, :] * s[None, :, :]).reshape(64, 128)
-                prod[q7 * 64 : q7 * 64 + 64, lanes] = p.astype(BF16)
+                twice = jnp.concatenate([s, s], axis=0).astype(BF16)
+                for k in range(4):
+                    two = [jnp.broadcast_to(a[r : r + 1], (8, 128)) for r in (2 * k, 2 * k + 1)]
+                    row = q7 * 64 + k * 16
+                    prod[row : row + 16, lanes] = jnp.concatenate(two, axis=0).astype(BF16) * twice
                 linear.append(a)
             prod[448:512, lanes] = jnp.concatenate(linear + linear[6:], axis=0).astype(BF16)
 
@@ -387,7 +390,7 @@
     stops = [
         jnp.where(early, jnp.where(z == 3, 1, 5 - z), 0),
         jnp.where(early, jnp.where(z < 2, 8, 6), 2),
-        jnp.where(early, 8, 6),
+        jnp.where(early, 8, 4),
     ]
 
     @pl.when(early)
@@ -414,9 +417,6 @@
     ]
     northward = copy(to_north, rs, send_h.at[2], recv_h.at[2], {"lat": north})
     southward = copy(to_south, rn, send_h.at[3], recv_h.at[3], {"lat": south})
-    for halo in halos:
-        halo.start()
-
     @pl.when(has_north)
     def _():
         northward.start()
@@ -442,11 +442,29 @@
     ]
     for hop in spread:
         hop.start()
+    for halo in halos:
+        halo.start()
     volume(stops[1], stops[2])
 
     @pl.when(early)
     def _():
         volume_product(dperm, trans, v_ref)
+
+    def faces(g, t, remote):
+        flux(g, t, remote, own, turn_ref, wf, terms)
+
+    def from_below(t, m):
+        return jnp.where(below_first, zero, pltpu.roll(own[5, t, m], 1, 1))
+
+    def from_above(t, m):
+        return jnp.where(above_last, zero, pltpu.roll(own[4, t, m], 127, 1))
+
+    def radial(t, carry):
+        faces(4, t, from_below)
+        faces(5, t, from_above)
+        return carry
+
+    lax.fori_loop(0, 3, radial, 0)
 
     for hop in spread:
         hop.wait_recv()
@@ -468,22 +486,6 @@
     def _():
         volume(stops[2], 8)
         volume_product(dperm, trans, v_ref)
-
-    def faces(g, t, remote):
-        flux(g, t, remote, own, turn_ref, wf, terms)
-
-    def from_below(t, m):
-        return jnp.where(below_first, zero, pltpu.roll(own[5, t, m], 1, 1))
-
-    def from_above(t, m):
-        return jnp.where(above_last, zero, pltpu.roll(own[4, t, m], 127, 1))
-
-    def radial(t, carry):
-        faces(4, t, from_below)
-        faces(5, t, from_above)
-        return carry
-
-    lax.fori_loop(0, 3, radial, 0)
 
     def inner_lon(index, carry):
         g = index // 2

time: 38.1 us -> 35.8 us (0.940)
  the two profiles are of different devices: /device:TPU:1 before, /device:TPU:6 now
where the time goes in v3:
time: 35.8 us; the launch traced here: 35.7 us
  Pallas kernels  35.7 us (100%)
    pallas_call x1, Pallas kernels, exchange(): pl.pallas_call(kernel, out_shape=[jax.ShapeDtypeStruct((3, 6, 36, 8, 128)...  33.3 us
    pallas_call x1, Pallas kernels, finished(): pl.pallas_call(finish_kernel, out_shape=jax.ShapeDtypeStruct((216, 3, 8,...  2.33 us

profile of v3, /device:TPU:6, one launch (start us, length us, event | category | flops | bytes accessed | tf_op | source)
XLA Modules:
  0.0 35.7 jit_solution(11372445235573637979)
XLA Ops:
  0.0 33.3 %shard_map.82 = (f32[3,6,36,8,128]{4,3,2,1,0:T(8,128)S(1)}, f32[3,1728,128]{2,1,0:T(8,128)S(1)}, f32[64,128]{1,0:T(8,128)S(1)}, f32[3,12,8,128]{3,2,1,0:T(8,128)S(1)}) custom-call(bf16[216,3,8,128]{3,2,1,0:T(8,128)(2,1)} %bitcast.8, bf16[216,3,8,128]{3,2,1,0:T(8,128)(2,1)} %bitcast.9, bf16[3,216,216]{2,1,0:T(8,128)(2,1)} %d_ref.1, bf16[192,8]{1,0:T(8,128)(2,1)} %bitcast.10, ...), custom_call_target="tpu_custom_call" | custom-call | tf_op jit(solution)/shard_map/pallas_call | solution.py:547
  33.3 2.3 %shard_map.83 = bf16[216,3,8,128]{3,2,1,0:T(8,128)(2,1)} custom-call(f32[3,6,36,8,128]{4,3,2,1,0:T(8,128)S(1)} %get-tuple-element.9.terms_in, f32[3,1728,128]{2,1,0:T(8,128)S(1)} %get-tuple-element.10.v_ref, f32[64,128]{1,0:T(8,128)S(1)} %get-tuple-element.11.zon_ref, f32[3,12,8,128]{3,2,1,0:T(8,128)S(1)} %get-tuple-element.12.swaps), custom_call_target="tpu_custom_call" | custom-call | tf_op jit(solution)/shard_map/pallas_call | solution.py:594
